TPU v7x, 32 devices: a whole 2x2x4 slice. The times are simulated.
32 devices in a mesh: arcs: 2 (over y), seg: 16 (over z, x, core).
Axes of the slice: x: 2, y: 2, z: 4, core: 2. Of those that a mesh axis runs over, the one named last changes fastest.
Arguments:
- pulses: bfloat16 [2, 8192, 256], P(None, ('arcs', 'seg')), parts along dimension 1, may hold values from -6 to 6
- fraction: float32 [8192], P(('arcs', 'seg')), parts along dimension 0, may hold values from 0 to 1
- gate_shift: int32 [8192], P(('arcs', 'seg')), parts along dimension 0, may hold values from 0 to 15
- aperture_start: int32 [4096], P(('arcs', 'seg')), parts along dimension 0, may hold values from 0 to 4095, as said below
- aperture_end: int32 [4096], P(('arcs', 'seg')), parts along dimension 0, may hold values from 257 to 4096, as said below
- doppler: float32 [4096], P(('arcs', 'seg')), parts along dimension 0, may hold values from -2000 to 2000
- chirp_rate: float32 [4096], P(('arcs', 'seg')), parts along dimension 0, may hold values from 2000 to 6000
Outputs:
- focused: bfloat16 [2, 4096, 256], P(None, ('arcs', 'seg')), parts along dimension 1
- multilook: float32 [4096, 256], P(('arcs', 'seg')), parts along dimension 0
There are 2 independent parts, one for each index of `arcs`. A program takes and returns all parts, laid end to end along the dimension named above; each array names one. Nothing has to cross between parts.
Inputs may be any that keep to these rules, and one draw needn't show every extreme that they name: aperture_start[w] >= (w // 128 - 4) * 256, with equality for some waveform; aperture_end[w] - aperture_start[w] >= 257. aperture_end[w] <= (w // 128 + 5) * 256, with equality for some waveform; aperture_start[w] < aperture_end[w].
All inputs are finite; a program needn't handle non-finite values.
Results may differ from a plain program's by a relative error of at most 0.0064.
Values may be sent and summed in bfloat16 or wider, within the bound.
A program may use at most 64 MiB of HBM per device.

v0:
```python
import jax
import jax.numpy as jnp
from jax import lax
from jax.sharding import PartitionSpec as P

G = 256
P_DEV = 256
REACH = 4
LOOK = 8
SHIFT_MAX = 16


def from_behind(array, axis, by):
    devices = lax.axis_size(axis)
    pairs = [(i, i + by) for i in range(devices) if 0 <= i + by < devices]
    return lax.ppermute(array, axis, pairs)


def padded(array, sides, width):
    for axis, dim in sides:
        devices, length = (lax.axis_size(axis), array.shape[dim])
        up = [(i, (i + 1) % devices) for i in range(devices - 1)]
        down = [(j, i) for i, j in up]
        last = lax.slice_in_dim(array, length - width, length, axis=dim)
        initial = lax.slice_in_dim(array, 0, width, axis=dim)
        before = lax.ppermute(last, axis, up)
        after = lax.ppermute(initial, axis, down)
        array = jnp.concatenate([before, array, after], axis=dim)
    return array


def migrate(pulses, fraction, gate_shift):
    widened = jnp.pad(pulses.astype(jnp.float32), ((0, 0), (0, 0), (0, SHIFT_MAX + 1)))
    blend = fraction[None, :, None]
    shift_col = gate_shift[None, :, None]
    result = jnp.zeros(pulses.shape, jnp.float32)
    for gate_step in range(SHIFT_MAX + 1):
        coeff = jnp.where(shift_col == gate_step, 1.0 - blend, 0.0) + jnp.where(
            shift_col + 1 == gate_step, blend, 0.0
        )
        result = result + coeff * widened[:, :, gate_step : gate_step + G]
    return result.astype(jnp.bfloat16)


def weights(first_pulse, last_pulse, doppler, chirp_rate, pulse_index):
    center = (first_pulse + last_pulse) // 2
    relative = (pulse_index[None, :] - center[:, None]).astype(jnp.float32) / float(REACH * P_DEV)
    phase_angle = chirp_rate[:, None] * relative * relative + doppler[:, None] * relative
    inside = (pulse_index[None, :] >= first_pulse[:, None]) & (
        pulse_index[None, :] < last_pulse[:, None]
    )
    amplitude = lax.rsqrt((last_pulse - first_pulse).astype(jnp.float32))[:, None]
    weight_re = jnp.where(inside, amplitude * jnp.cos(phase_angle), 0.0).astype(jnp.bfloat16)
    weight_im = jnp.where(inside, amplitude * jnp.sin(phase_angle), 0.0).astype(jnp.bfloat16)
    return (weight_re, weight_im)


def focus_block(weight_re, weight_im, block_data):
    real_part = jnp.dot(weight_re, block_data[0], preferred_element_type=jnp.float32) - jnp.dot(
        weight_im, block_data[1], preferred_element_type=jnp.float32
    )
    imag_part = jnp.dot(weight_re, block_data[1], preferred_element_type=jnp.float32) + jnp.dot(
        weight_im, block_data[0], preferred_element_type=jnp.float32
    )
    return jnp.stack([real_part, imag_part])


def settle(term):
    rounded = lax.optimization_barrier(term.astype(jnp.bfloat16))
    return rounded.astype(jnp.float32)


def shards(pulses, fraction, gate_shift, aperture_start, aperture_end, doppler, chirp_rate):
    device = lax.axis_index("seg")
    pulse_count = pulses.shape[1]
    wave_count = aperture_start.shape[0]
    local_index = jnp.arange(pulse_count, dtype=jnp.int32)
    migrated = migrate(pulses, fraction, gate_shift)

    def own_focus(block_data, block_owner):
        weight_re, weight_im = weights(
            aperture_start,
            aperture_end,
            doppler,
            chirp_rate,
            block_owner * pulse_count + local_index,
        )
        return focus_block(weight_re, weight_im, block_data)

    summed = settle(own_focus(migrated, device))
    for offset in range(1, REACH + 1):
        from_lower = from_behind(migrated, "seg", offset)
        from_upper = from_behind(migrated, "seg", -offset)
        summed = (
            summed
            + settle(own_focus(from_lower, device - offset))
            + settle(own_focus(from_upper, device + offset))
        )
    power_sum = summed[0] * summed[0] + summed[1] * summed[1]
    power_pad = padded(power_sum.astype(jnp.bfloat16), (("seg", 0),), LOOK).astype(power_sum.dtype)
    looked = jnp.zeros((wave_count, power_sum.shape[1]), jnp.float32)
    for shift_row in range(2 * LOOK + 1):
        looked = looked + power_pad[shift_row : shift_row + wave_count]
    multilook = looked / float(2 * LOOK + 1)
    return (summed.astype(jnp.bfloat16), multilook)


def solution(mesh):
    return jax.shard_map(
        shards,
        mesh=mesh,
        in_specs=(
            P(None, ("arcs", "seg"), None),
            P(("arcs", "seg")),
            P(("arcs", "seg")),
            P(("arcs", "seg")),
            P(("arcs", "seg")),
            P(("arcs", "seg")),
            P(("arcs", "seg")),
        ),
        out_specs=(P(None, ("arcs", "seg"), None), P(("arcs", "seg"), None)),
        check_vma=False,
    )
```

profile of v0, /device:TPU:3, one launch (start us, length us, event | category | flops | bytes accessed | tf_op | source)
XLA Modules:
  0.0 66.9 jit_solution(14454943047217304032)
XLA Ops:
  0.6 1.0 %convert_element_type.151 = f32[2,256,256]{2,1,0:T(8,128)S(1)} convert(bf16[2,256,256]{2,1,0:T(8,128)(2,1)} %param.7) | non-fusion elementwise | flops 131072 | bytes 786432 | tf_op jit(solution)/shard_map/convert_element_type | solution.py:33
  1.7 3.0 %fusion.68 = bf16[2,256,256]{2,1,0:T(8,128)(2,1)S(1)} fusion(f32[2,256,256]{2,1,0:T(8,128)S(1)} %convert_element_type.151, f32[256]{0:T(256)S(1)} %get-tuple-element.21, f32[256]{0:T(256)S(1)} %get-tuple-element.22, f32[256]{0:T(256)S(1)} %get-tuple-element.20, f32[256]{0:T(256)S(1)} %get-tuple-element.7, f32[256]{0:T(256)S(1)} %get-tuple-element.8, ...), kind=kLoop, calls=%fused_computation.102 | loop fusion | flops 4456448 | bytes 803840 | tf_op jit(solution)/shard_map/convert_element_type | solution.py:42
  4.7 3.7 %collective-permute-start = (bf16[2,256,256]{2,1,0:T(8,128)(2,1)S(1)}, bf16[2,256,256]{2,1,0:T(8,128)(2,1)S(1)}, u32[]{:S(2)}, u32[]{:S(2)}) collective-permute-start(bf16[2,256,256]{2,1,0:T(8,128)(2,1)S(1)} %fusion.68), channel_id=1, source_target_pairs={{0,1},{1,2},{2,3},{3,4},{4,5},{5,6},{6,7},{7,8},{8,9},{9,10},{10,1... | collective-permute-start | bytes 786440 | tf_op jit(solution)/shard_map/ppermute | solution.py:16
  8.5 1.9 %collective-permute-start.1 = (bf16[2,256,256]{2,1,0:T(8,128)(2,1)S(1)}, bf16[2,256,256]{2,1,0:T(8,128)(2,1)S(1)}, u32[]{:S(2)}, u32[]{:S(2)}) collective-permute-start(bf16[2,256,256]{2,1,0:T(8,128)(2,1)S(1)} %fusion.68), channel_id=1, source_target_pairs={{1,0},{2,1},{3,2},{4,3},{5,4},{6,5},{7,6},{8,7},{9,8},{10,9},{11,1... | collective-permute-start | bytes 786440 | tf_op jit(solution)/shard_map/ppermute | solution.py:16
  10.4 3.1 %collective-permute-start.2 = (bf16[2,256,256]{2,1,0:T(8,128)(2,1)S(1)}, bf16[2,256,256]{2,1,0:T(8,128)(2,1)S(1)}, u32[]{:S(2)}, u32[]{:S(2)}) collective-permute-start(bf16[2,256,256]{2,1,0:T(8,128)(2,1)S(1)} %fusion.68), channel_id=1, source_target_pairs={{0,2},{1,3},{2,4},{3,5},{4,6},{5,7},{6,8},{7,9},{8,10},{9,11},{10,... | collective-permute-start | bytes 786440 | tf_op jit(solution)/shard_map/ppermute | solution.py:16
  13.5 2.2 %collective-permute-start.3 = (bf16[2,256,256]{2,1,0:T(8,128)(2,1)S(1)}, bf16[2,256,256]{2,1,0:T(8,128)(2,1)S(1)}, u32[]{:S(2)}, u32[]{:S(2)}) collective-permute-start(bf16[2,256,256]{2,1,0:T(8,128)(2,1)S(1)} %fusion.68), channel_id=1, source_target_pairs={{2,0},{3,1},{4,2},{5,3},{6,4},{7,5},{8,6},{9,7},{10,8},{11,9},{12,... | collective-permute-start | bytes 786440 | tf_op jit(solution)/shard_map/ppermute | solution.py:16
  15.7 4.7 %collective-permute-start.4 = (bf16[2,256,256]{2,1,0:T(8,128)(2,1)S(1)}, bf16[2,256,256]{2,1,0:T(8,128)(2,1)S(1)}, u32[]{:S(2)}, u32[]{:S(2)}) collective-permute-start(bf16[2,256,256]{2,1,0:T(8,128)(2,1)S(1)} %fusion.68), channel_id=1, source_target_pairs={{0,3},{1,4},{2,5},{3,6},{4,7},{5,8},{6,9},{7,10},{8,11},{9,12},{10... | collective-permute-start | bytes 786440 | tf_op jit(solution)/shard_map/ppermute | solution.py:16
  23.1 0.7 %fusion.34 = bf16[1,128,256]{2,1,0:T(8,128)(2,1)S(1)} fusion(f32[128,256]{1,0:T(8,128)S(1)} %fusion.73, bf16[2,256,256]{2,1,0:T(8,128)(2,1)S(1)} %fusion.68, f32[128]{0:T(128)S(1)} %get-tuple-element.24, f32[128]{0:T(128)S(1)} %broadcast_multiply_fusion.1, s32[128]{0:T(128)S(1)} %and_select_fusion, f32[128]{0:T(128)S(1)} %get-tuple-element.23, ...), kind=kOutput, calls=%fused_computation.68 | convolution fusion | flops 17268736 | bytes 331776 | tf_op jit(solution)/shard_map/dot_general | solution.py:62
  23.8 0.7 %fusion.35 = bf16[1,128,256]{2,1,0:T(8,128)(2,1)S(1)} fusion(f32[128,256]{1,0:T(8,128)S(1)} %fusion.72, bf16[2,256,256]{2,1,0:T(8,128)(2,1)S(1)} %fusion.68, f32[128]{0:T(128)S(1)} %get-tuple-element.24, f32[128]{0:T(128)S(1)} %broadcast_multiply_fusion.1, s32[128]{0:T(128)S(1)} %and_select_fusion, f32[128]{0:T(128)S(1)} %get-tuple-element.23, ...), kind=kOutput, calls=%fused_computation.69 | convolution fusion | flops 17268736 | bytes 331776 | tf_op jit(solution)/shard_map/dot_general | solution.py:59
  24.6 1.9 %collective-permute-start.5 = (bf16[2,256,256]{2,1,0:T(8,128)(2,1)S(1)}, bf16[2,256,256]{2,1,0:T(8,128)(2,1)S(1)}, u32[]{:S(2)}, u32[]{:S(2)}) collective-permute-start(bf16[2,256,256]{2,1,0:T(8,128)(2,1)S(1)} %fusion.68), channel_id=1, source_target_pairs={{3,0},{4,1},{5,2},{6,3},{7,4},{8,5},{9,6},{10,7},{11,8},{12,9},{13... | collective-permute-start | bytes 786440 | tf_op jit(solution)/shard_map/ppermute | solution.py:16
  26.5 0.7 %fusion.74 = f32[128,256]{1,0:T(8,128)S(1)} fusion(bf16[2,256,256]{2,1,0:T(8,128)(2,1)S(1)} %collective-permute-done, s32[256]{0:T(256)S(1)} %iota_add_fusion.7, f32[128]{0:T(128)S(1)} %get-tuple-element.24, f32[128]{0:T(128)S(1)} %broadcast_multiply_fusion.1, s32[128]{0:T(128)S(1)} %and_select_fusion, f32[128]{0:T(128)S(1)} %get-tuple-element.23, ...), kind=kOutput, calls=%fused_computation.190 | convolution fusion | flops 17203200 | bytes 266240 | tf_op jit(solution)/shard_map/dot_general | solution.py:62
  27.2 0.7 %fusion.75 = f32[128,256]{1,0:T(8,128)S(1)} fusion(bf16[2,256,256]{2,1,0:T(8,128)(2,1)S(1)} %collective-permute-done, s32[256]{0:T(256)S(1)} %iota_add_fusion.7, f32[128]{0:T(128)S(1)} %get-tuple-element.24, f32[128]{0:T(128)S(1)} %broadcast_multiply_fusion.1, s32[128]{0:T(128)S(1)} %and_select_fusion, f32[128]{0:T(128)S(1)} %get-tuple-element.23, ...), kind=kOutput, calls=%fused_computation.191 | convolution fusion | flops 17203200 | bytes 266240 | tf_op jit(solution)/shard_map/dot_general | solution.py:59
  27.8 3.5 %collective-permute-start.6 = (bf16[2,256,256]{2,1,0:T(8,128)(2,1)S(1)}, bf16[2,256,256]{2,1,0:T(8,128)(2,1)S(1)}, u32[]{:S(2)}, u32[]{:S(2)}) collective-permute-start(bf16[2,256,256]{2,1,0:T(8,128)(2,1)S(1)} %fusion.68), channel_id=1, source_target_pairs={{0,4},{1,5},{2,6},{3,7},{4,8},{5,9},{6,10},{7,11},{8,12},{9,13},{1... | collective-permute-start | bytes 786440 | tf_op jit(solution)/shard_map/ppermute | solution.py:16
  31.4 0.7 %fusion.76 = f32[128,256]{1,0:T(8,128)S(1)} fusion(bf16[2,256,256]{2,1,0:T(8,128)(2,1)S(1)} %collective-permute-done.1, s32[256]{0:T(256)S(1)} %iota_add_fusion.6, f32[128]{0:T(128)S(1)} %get-tuple-element.24, f32[128]{0:T(128)S(1)} %broadcast_multiply_fusion.1, s32[128]{0:T(128)S(1)} %and_select_fusion, f32[128]{0:T(128)S(1)} %get-tuple-element.23, ...), kind=kOutput, calls=%fused_computation.192 | convolution fusion | flops 17203200 | bytes 266240 | tf_op jit(solution)/shard_map/dot_general | solution.py:62
  32.1 0.7 %fusion.77 = f32[128,256]{1,0:T(8,128)S(1)} fusion(bf16[2,256,256]{2,1,0:T(8,128)(2,1)S(1)} %collective-permute-done.1, s32[256]{0:T(256)S(1)} %iota_add_fusion.6, f32[128]{0:T(128)S(1)} %get-tuple-element.24, f32[128]{0:T(128)S(1)} %broadcast_multiply_fusion.1, s32[128]{0:T(128)S(1)} %and_select_fusion, f32[128]{0:T(128)S(1)} %get-tuple-element.23, ...), kind=kOutput, calls=%fused_computation.193 | convolution fusion | flops 17203200 | bytes 266240 | tf_op jit(solution)/shard_map/dot_general | solution.py:59
  33.4 0.7 %fusion.33 = bf16[1,128,256]{2,1,0:T(8,128)(2,1)S(1)} fusion(f32[128,256]{1,0:T(8,128)S(1)} %fusion.75, bf16[2,256,256]{2,1,0:T(8,128)(2,1)S(1)} %collective-permute-done, s32[256]{0:T(256)S(1)} %iota_add_fusion.7, f32[128]{0:T(128)S(1)} %get-tuple-element.24, f32[128]{0:T(128)S(1)} %broadcast_multiply_fusion.1, s32[128]{0:T(128)S(1)} %and_select_fusion, ...), kind=kOutput, calls=%fused_computation.67 | convolution fusion | flops 17268736 | bytes 331776 | tf_op jit(solution)/shard_map/dot_general | solution.py:59
  35.5 1.5 %collective-permute-start.7 = (bf16[2,256,256]{2,1,0:T(8,128)(2,1)S(1)}, bf16[2,256,256]{2,1,0:T(8,128)(2,1)S(1)}, u32[]{:S(2)}, u32[]{:S(2)}) collective-permute-start(bf16[2,256,256]{2,1,0:T(8,128)(2,1)S(1)} %fusion.68), channel_id=1, source_target_pairs={{4,0},{5,1},{6,2},{7,3},{8,4},{9,5},{10,6},{11,7},{12,8},{13,9},{1... | collective-permute-start | bytes 786440 | tf_op jit(solution)/shard_map/ppermute | solution.py:16
  36.9 0.7 %fusion.78 = f32[128,256]{1,0:T(8,128)S(1)} fusion(bf16[2,256,256]{2,1,0:T(8,128)(2,1)S(1)} %collective-permute-done.2, s32[256]{0:T(256)S(1)} %iota_add_fusion.5, f32[128]{0:T(128)S(1)} %get-tuple-element.24, f32[128]{0:T(128)S(1)} %broadcast_multiply_fusion.1, s32[128]{0:T(128)S(1)} %and_select_fusion, f32[128]{0:T(128)S(1)} %get-tuple-element.23, ...), kind=kOutput, calls=%fused_computation.194 | convolution fusion | flops 17203200 | bytes 266240 | tf_op jit(solution)/shard_map/dot_general | solution.py:62
  37.6 0.7 %fusion.79 = f32[128,256]{1,0:T(8,128)S(1)} fusion(bf16[2,256,256]{2,1,0:T(8,128)(2,1)S(1)} %collective-permute-done.2, s32[256]{0:T(256)S(1)} %iota_add_fusion.5, f32[128]{0:T(128)S(1)} %get-tuple-element.24, f32[128]{0:T(128)S(1)} %broadcast_multiply_fusion.1, s32[128]{0:T(128)S(1)} %and_select_fusion, f32[128]{0:T(128)S(1)} %get-tuple-element.23, ...), kind=kOutput, calls=%fused_computation.195 | convolution fusion | flops 17203200 | bytes 266240 | tf_op jit(solution)/shard_map/dot_general | solution.py:59
  38.3 0.7 %fusion.80 = f32[128,256]{1,0:T(8,128)S(1)} fusion(bf16[2,256,256]{2,1,0:T(8,128)(2,1)S(1)} %collective-permute-done.3, s32[256]{0:T(256)S(1)} %iota_add_fusion.4, f32[128]{0:T(128)S(1)} %get-tuple-element.24, f32[128]{0:T(128)S(1)} %broadcast_multiply_fusion.1, s32[128]{0:T(128)S(1)} %and_select_fusion, f32[128]{0:T(128)S(1)} %get-tuple-element.23, ...), kind=kOutput, calls=%fused_computation.196 | convolution fusion | flops 17203200 | bytes 266240 | tf_op jit(solution)/shard_map/dot_general | solution.py:62
  39.0 0.7 %fusion.81 = f32[128,256]{1,0:T(8,128)S(1)} fusion(bf16[2,256,256]{2,1,0:T(8,128)(2,1)S(1)} %collective-permute-done.3, s32[256]{0:T(256)S(1)} %iota_add_fusion.4, f32[128]{0:T(128)S(1)} %get-tuple-element.24, f32[128]{0:T(128)S(1)} %broadcast_multiply_fusion.1, s32[128]{0:T(128)S(1)} %and_select_fusion, f32[128]{0:T(128)S(1)} %get-tuple-element.23, ...), kind=kOutput, calls=%fused_computation.197 | convolution fusion | flops 17203200 | bytes 266240 | tf_op jit(solution)/shard_map/dot_general | solution.py:59
  39.7 0.7 %fusion.82 = f32[128,256]{1,0:T(8,128)S(1)} fusion(bf16[2,256,256]{2,1,0:T(8,128)(2,1)S(1)} %collective-permute-done.4, s32[256]{0:T(256)S(1)} %iota_add_fusion.3, f32[128]{0:T(128)S(1)} %get-tuple-element.24, f32[128]{0:T(128)S(1)} %broadcast_multiply_fusion.1, s32[128]{0:T(128)S(1)} %and_select_fusion, f32[128]{0:T(128)S(1)} %get-tuple-element.23, ...), kind=kOutput, calls=%fused_computation.198 | convolution fusion | flops 17203200 | bytes 266240 | tf_op jit(solution)/shard_map/dot_general | solution.py:62
  40.4 0.7 %fusion.83 = f32[128,256]{1,0:T(8,128)S(1)} fusion(bf16[2,256,256]{2,1,0:T(8,128)(2,1)S(1)} %collective-permute-done.4, s32[256]{0:T(256)S(1)} %iota_add_fusion.3, f32[128]{0:T(128)S(1)} %get-tuple-element.24, f32[128]{0:T(128)S(1)} %broadcast_multiply_fusion.1, s32[128]{0:T(128)S(1)} %and_select_fusion, f32[128]{0:T(128)S(1)} %get-tuple-element.23, ...), kind=kOutput, calls=%fused_computation.199 | convolution fusion | flops 17203200 | bytes 266240 | tf_op jit(solution)/shard_map/dot_general | solution.py:59
  45.2 0.7 %fusion.84 = f32[128,256]{1,0:T(8,128)S(1)} fusion(bf16[2,256,256]{2,1,0:T(8,128)(2,1)S(1)} %collective-permute-done.5, s32[256]{0:T(256)S(1)} %iota_add_fusion.2, f32[128]{0:T(128)S(1)} %get-tuple-element.24, f32[128]{0:T(128)S(1)} %broadcast_multiply_fusion.1, s32[128]{0:T(128)S(1)} %and_select_fusion, f32[128]{0:T(128)S(1)} %get-tuple-element.23, ...), kind=kOutput, calls=%fused_computation.200 | convolution fusion | flops 17203200 | bytes 266240 | tf_op jit(solution)/shard_map/dot_general | solution.py:62
  46.5 0.7 %fusion.87 = f32[128,256]{1,0:T(8,128)S(1)} fusion(bf16[2,256,256]{2,1,0:T(8,128)(2,1)S(1)} %collective-permute-done.6, s32[256]{0:T(256)S(1)} %iota_add_fusion.1, f32[128]{0:T(128)S(1)} %get-tuple-element.24, f32[128]{0:T(128)S(1)} %broadcast_multiply_fusion.1, s32[128]{0:T(128)S(1)} %and_select_fusion, f32[128]{0:T(128)S(1)} %get-tuple-element.23, ...), kind=kOutput, calls=%fused_computation.203 | convolution fusion | flops 17203200 | bytes 266240 | tf_op jit(solution)/shard_map/dot_general | solution.py:59
  47.2 0.7 %fusion.86 = f32[128,256]{1,0:T(8,128)S(1)} fusion(bf16[2,256,256]{2,1,0:T(8,128)(2,1)S(1)} %collective-permute-done.6, s32[256]{0:T(256)S(1)} %iota_add_fusion.1, f32[128]{0:T(128)S(1)} %get-tuple-element.24, f32[128]{0:T(128)S(1)} %broadcast_multiply_fusion.1, s32[128]{0:T(128)S(1)} %and_select_fusion, f32[128]{0:T(128)S(1)} %get-tuple-element.23, ...), kind=kOutput, calls=%fused_computation.202 | convolution fusion | flops 17203200 | bytes 266240 | tf_op jit(solution)/shard_map/dot_general | solution.py:62
  51.3 0.7 %fusion.88 = f32[128,256]{1,0:T(8,128)S(1)} fusion(bf16[2,256,256]{2,1,0:T(8,128)(2,1)S(1)} %collective-permute-done.7, s32[256]{0:T(256)S(1)} %iota_add_fusion, f32[128]{0:T(128)S(1)} %get-tuple-element.24, f32[128]{0:T(128)S(1)} %broadcast_multiply_fusion.1, s32[128]{0:T(128)S(1)} %and_select_fusion, f32[128]{0:T(128)S(1)} %get-tuple-element.23, ...), kind=kOutput, calls=%fused_computation.204 | convolution fusion | flops 17203200 | bytes 266240 | tf_op jit(solution)/shard_map/dot_general | solution.py:62
  53.4 0.8 %fusion.179 = (bf16[2,128,256]{2,1,0:T(8,128)(2,1)}, f32[2,128,256]{2,1,0:T(8,128)S(1)}) fusion(bf16[2,128,256]{2,1,0:T(8,128)(2,1)S(1)} %pad_maximum_fusion.8, bf16[2,128,256]{2,1,0:T(8,128)(2,1)S(1)} %pad_maximum_fusion.7, bf16[2,128,256]{2,1,0:T(8,128)(2,1)S(1)} %pad_maximum_fusion.6, bf16[2,128,256]{2,1,0:T(8,128)(2,1)S(1)} %pad_maximum_fusion.5, ...), kind=kLoop, calls=%fused_computation.350 | loop fusion | flops 1179648 | bytes 1572864 | tf_op jit(solution)/shard_map/convert_element_type | solution.py:105
  54.2 6.0 %collective-permute-start.8 = (bf16[8,256]{1,0:T(8,128)(2,1)S(1)}, bf16[8,256]{1,0:T(8,128)(2,1)S(1)}, u32[]{:S(2)}, u32[]{:S(2)}) collective-permute-start(bf16[8,256]{1,0:T(8,128)(2,1)S(1)} %get-tuple-element.4), channel_id=1, source_target_pairs={{0,1},{1,2},{2,3},{3,4},{4,5},{5,6},{6,7},{7,8},{8,9},{9,10},{10,1... | collective-permute-start | bytes 12296 | tf_op jit(solution)/shard_map/ppermute | solution.py:26
  60.3 1.9 %collective-permute-start.9 = (bf16[8,256]{1,0:T(8,128)(2,1)S(1)}, bf16[8,256]{1,0:T(8,128)(2,1)S(1)}, u32[]{:S(2)}, u32[]{:S(2)}) collective-permute-start(bf16[8,256]{1,0:T(8,128)(2,1)S(1)} %get-tuple-element.5), channel_id=1, source_target_pairs={{1,0},{2,1},{3,2},{4,3},{5,4},{6,5},{7,6},{8,7},{9,8},{10,9},{11,1... | collective-permute-start | bytes 12296 | tf_op jit(solution)/shard_map/ppermute | solution.py:27
  62.2 3.9 %collective-permute-done.9 = bf16[8,256]{1,0:T(8,128)(2,1)S(1)} collective-permute-done((bf16[8,256]{1,0:T(8,128)(2,1)S(1)}, bf16[8,256]{1,0:T(8,128)(2,1)S(1)}, u32[]{:S(2)}, u32[]{:S(2)}) %collective-permute-start.9) | collective-permute-done | bytes 4128 | tf_op jit(solution)/shard_map/ppermute | solution.py:27
  66.1 0.8 %fusion.69 = f32[128,256]{1,0:T(8,128)} fusion(f32[144,256]{1,0:T(8,128)S(1)} %maximum_convert_fusion), kind=kLoop, calls=%fused_computation.105 | loop fusion | flops 557056 | bytes 2359296 | tf_op jit(solution)/shard_map/div | solution.py:104
  (66 shorter events, 14.4 us)
Async XLA Ops:
  0.6 1.0 %copy-start.1 = (f32[256]{0:T(256)S(1)}, f32[256]{0:T(256)}, u32[]{:S(2)}) copy-start(f32[256]{0:T(256)} %param.8) | copy-start | bytes 3076
  0.6 1.0 %copy-start = (s32[256]{0:T(256)S(1)}, s32[256]{0:T(256)}, u32[]{:S(2)}) copy-start(s32[256]{0:T(256)} %param.9) | copy-start | bytes 3076
  4.7 15.7 %copy-start.3 = (s32[128]{0:T(128)S(1)}, s32[128]{0:T(128)}, u32[]{:S(2)}) copy-start(s32[128]{0:T(128)} %param.11) | copy-start | bytes 1540
  4.7 15.7 %copy-start.4 = (s32[128]{0:T(128)S(1)}, s32[128]{0:T(128)}, u32[]{:S(2)}) copy-start(s32[128]{0:T(128)} %param.10) | copy-start | bytes 1540
  4.7 19.8 %collective-permute-start = (bf16[2,256,256]{2,1,0:T(8,128)(2,1)S(1)}, bf16[2,256,256]{2,1,0:T(8,128)(2,1)S(1)}, u32[]{:S(2)}, u32[]{:S(2)}) collective-permute-start(bf16[2,256,256]{2,1,0:T(8,128)(2,1)S(1)} %fusion.68), channel_id=1, source_target_pairs={{0,1},{1,2},{2,3},{3,4},{4,5},{5,6},{6,7},{7,8},{8,9},{9,10},{10,1... | collective-permute-start | bytes 786440 | tf_op jit(solution)/shard_map/ppermute | solution.py:16
  8.5 19.4 %collective-permute-start.1 = (bf16[2,256,256]{2,1,0:T(8,128)(2,1)S(1)}, bf16[2,256,256]{2,1,0:T(8,128)(2,1)S(1)}, u32[]{:S(2)}, u32[]{:S(2)}) collective-permute-start(bf16[2,256,256]{2,1,0:T(8,128)(2,1)S(1)} %fusion.68), channel_id=1, source_target_pairs={{1,0},{2,1},{3,2},{4,3},{5,4},{6,5},{7,6},{8,7},{9,8},{10,9},{11,1... | collective-permute-start | bytes 786440 | tf_op jit(solution)/shard_map/ppermute | solution.py:16
  10.4 25.0 %collective-permute-start.2 = (bf16[2,256,256]{2,1,0:T(8,128)(2,1)S(1)}, bf16[2,256,256]{2,1,0:T(8,128)(2,1)S(1)}, u32[]{:S(2)}, u32[]{:S(2)}) collective-permute-start(bf16[2,256,256]{2,1,0:T(8,128)(2,1)S(1)} %fusion.68), channel_id=1, source_target_pairs={{0,2},{1,3},{2,4},{3,5},{4,6},{5,7},{6,8},{7,9},{8,10},{9,11},{10,... | collective-permute-start | bytes 786440 | tf_op jit(solution)/shard_map/ppermute | solution.py:16
  13.5 24.8 %collective-permute-start.3 = (bf16[2,256,256]{2,1,0:T(8,128)(2,1)S(1)}, bf16[2,256,256]{2,1,0:T(8,128)(2,1)S(1)}, u32[]{:S(2)}, u32[]{:S(2)}) collective-permute-start(bf16[2,256,256]{2,1,0:T(8,128)(2,1)S(1)} %fusion.68), channel_id=1, source_target_pairs={{2,0},{3,1},{4,2},{5,3},{6,4},{7,5},{8,6},{9,7},{10,8},{11,9},{12,... | collective-permute-start | bytes 786440 | tf_op jit(solution)/shard_map/ppermute | solution.py:16
  15.7 24.0 %collective-permute-start.4 = (bf16[2,256,256]{2,1,0:T(8,128)(2,1)S(1)}, bf16[2,256,256]{2,1,0:T(8,128)(2,1)S(1)}, u32[]{:S(2)}, u32[]{:S(2)}) collective-permute-start(bf16[2,256,256]{2,1,0:T(8,128)(2,1)S(1)} %fusion.68), channel_id=1, source_target_pairs={{0,3},{1,4},{2,5},{3,6},{4,7},{5,8},{6,9},{7,10},{8,11},{9,12},{10... | collective-permute-start | bytes 786440 | tf_op jit(solution)/shard_map/ppermute | solution.py:16
  20.4 0.7 copy-start.2
  21.1 0.7 copy-start.5
  24.6 20.6 %collective-permute-start.5 = (bf16[2,256,256]{2,1,0:T(8,128)(2,1)S(1)}, bf16[2,256,256]{2,1,0:T(8,128)(2,1)S(1)}, u32[]{:S(2)}, u32[]{:S(2)}) collective-permute-start(bf16[2,256,256]{2,1,0:T(8,128)(2,1)S(1)} %fusion.68), channel_id=1, source_target_pairs={{3,0},{4,1},{5,2},{6,3},{7,4},{8,5},{9,6},{10,7},{11,8},{12,9},{13... | collective-permute-start | bytes 786440 | tf_op jit(solution)/shard_map/ppermute | solution.py:16
  27.8 18.7 %collective-permute-start.6 = (bf16[2,256,256]{2,1,0:T(8,128)(2,1)S(1)}, bf16[2,256,256]{2,1,0:T(8,128)(2,1)S(1)}, u32[]{:S(2)}, u32[]{:S(2)}) collective-permute-start(bf16[2,256,256]{2,1,0:T(8,128)(2,1)S(1)} %fusion.68), channel_id=1, source_target_pairs={{0,4},{1,5},{2,6},{3,7},{4,8},{5,9},{6,10},{7,11},{8,12},{9,13},{1... | collective-permute-start | bytes 786440 | tf_op jit(solution)/shard_map/ppermute | solution.py:16
  35.5 15.2 %collective-permute-start.7 = (bf16[2,256,256]{2,1,0:T(8,128)(2,1)S(1)}, bf16[2,256,256]{2,1,0:T(8,128)(2,1)S(1)}, u32[]{:S(2)}, u32[]{:S(2)}) collective-permute-start(bf16[2,256,256]{2,1,0:T(8,128)(2,1)S(1)} %fusion.68), channel_id=1, source_target_pairs={{4,0},{5,1},{6,2},{7,3},{8,4},{9,5},{10,6},{11,7},{12,8},{13,9},{1... | collective-permute-start | bytes 786440 | tf_op jit(solution)/shard_map/ppermute | solution.py:16
  54.2 8.0 %collective-permute-start.8 = (bf16[8,256]{1,0:T(8,128)(2,1)S(1)}, bf16[8,256]{1,0:T(8,128)(2,1)S(1)}, u32[]{:S(2)}, u32[]{:S(2)}) collective-permute-start(bf16[8,256]{1,0:T(8,128)(2,1)S(1)} %get-tuple-element.4), channel_id=1, source_target_pairs={{0,1},{1,2},{2,3},{3,4},{4,5},{5,6},{6,7},{7,8},{8,9},{9,10},{10,1... | collective-permute-start | bytes 12296 | tf_op jit(solution)/shard_map/ppermute | solution.py:26
  60.3 5.8 %collective-permute-start.9 = (bf16[8,256]{1,0:T(8,128)(2,1)S(1)}, bf16[8,256]{1,0:T(8,128)(2,1)S(1)}, u32[]{:S(2)}, u32[]{:S(2)}) collective-permute-start(bf16[8,256]{1,0:T(8,128)(2,1)S(1)} %get-tuple-element.5), channel_id=1, source_target_pairs={{1,0},{2,1},{3,2},{4,3},{5,4},{6,5},{7,6},{8,7},{9,8},{10,9},{11,1... | collective-permute-start | bytes 12296 | tf_op jit(solution)/shard_map/ppermute | solution.py:27
where the time goes:
time: 67.3 us; the launch traced here: 66.9 us
  starting transfers between devices  30.5 us (45%)
  matrix products  24.4 us (36%)
  other arithmetic  5.89 us (9%)
  waiting for transfers between devices  3.88 us (6%)
  local copies, waits for them, and re-layouts  1.31 us (2%)
  between operations  1.01 us (2%)
    ppermute x8, starting transfers between devices, from_behind(): return lax.ppermute(array, axis, pairs)  22.5 us
    dot_general x9, matrix products, focus_block(): jnp.dot(weight_im, block_data[0], preferred_element_type=jnp.float32)  6.11 us
    dot_general x9, matrix products, focus_block(): jnp.dot(weight_im, block_data[1], preferred_element_type=jnp.float32)  6.1 us
    dot_general x9, matrix products, focus_block(): jnp.dot(weight_re, block_data[0], preferred_element_type=jnp.float32)  6.08 us
    dot_general x9, matrix products, focus_block(): jnp.dot(weight_re, block_data[1], preferred_element_type=jnp.float32)  6.07 us
    ppermute x1, starting transfers between devices, padded(): before = lax.ppermute(last, axis, up)  6.01 us
    ppermute x1, waiting for transfers between devices, padded(): after = lax.ppermute(initial, axis, down)  3.86 us
    convert_element_type x1, other arithmetic, migrate(): return result.astype(jnp.bfloat16)  3.01 us
  transfers between devices with their start and end apart: 10, of which 1 were waited for; matrix products, arithmetic and copies ran while one was open for 33% of the time, Pallas kernels for 0%

commit v1 on v0

v1 whole, which is shorter than its diff:
```python
import functools
import math

import jax
import jax.numpy as jnp
from jax import lax
from jax.experimental import pallas as pl
from jax.experimental.pallas import tpu as pltpu
from jax.sharding import PartitionSpec as P

REACH = 4
LOOK = 8
SHIFT_BITS = 4
ROWS = 32
MESH = pl.DeviceIdType.MESH

SIN = (3.141592640130708, -5.167710083507871, 2.550077523214076, -0.5982912856170641, 0.07765766029898877)
COS = (0.9999999532476084, -4.93479283061964, 4.058411352862407, -1.3318765680796267, 0.21968961109548557)


def horner(coefs, u):
    result = coefs[-1] * u + coefs[-2]
    for c in coefs[-3::-1]:
        result = result * u + c
    return result


def kernel(n, pulses_ref, gates_ref, params_ref, focus_ref, look_ref,
           mig, wts, cols, gcols, pbuf, sendb, recvb, acc, power,
           psend, precv, tsend, trecv, hsend, hrecv):
    me = lax.axis_index("seg")
    pulse_count, gates = pulses_ref.shape[1:]
    waves = params_ref.shape[1]
    scale = 1.0 / float(REACH * pulse_count)
    slots = 2 * REACH

    def offset(i):
        mag = REACH - lax.div(i, 2)
        return mag * (1 - 2 * lax.rem(i, 2))

    def exists(d):
        return (d >= 0) & (d < n)

    def each(body):
        def step(i, carry):
            body(i, offset(i))
            return carry
        lax.fori_loop(0, slots, step, 0)

    barrier = pltpu.get_barrier_semaphore()

    def greet(i, o):
        @pl.when(exists(me + o))
        def _():
            pl.semaphore_signal(barrier, inc=1, device_id={"seg": me + o}, device_id_type=MESH)

    each(greet)
    gcols[...] = gates_ref[...].T
    lane = lax.broadcasted_iota(jnp.int32, (ROWS, gates), 1)

    def migrate_rows(q, carry):
        rows = pl.ds(pl.multiple_of(q * ROWS, ROWS), ROWS)
        frac = gcols[rows, 0:1]
        shift = gcols[rows, 1:2].astype(jnp.int32)
        for c in range(2):
            x = pulses_ref[c, rows, :].astype(jnp.float32)
            nxt = jnp.where(lane == gates - 1, 0.0, pltpu.roll(x, gates - 1, 1))
            z = (1.0 - frac) * x + frac * nxt
            for b in range(SHIFT_BITS):
                z = jnp.where((shift & (1 << b)) != 0, pltpu.roll(z, gates - (1 << b), 1), z)
            z = jnp.where(lane + shift < gates, z, 0.0)
            mig[rows, c * gates:(c + 1) * gates] = z.astype(jnp.bfloat16)
        return carry

    pl.semaphore_wait(barrier, jnp.minimum(me, REACH) + jnp.minimum(n - 1 - me, REACH))

    def params_copy(i, target):
        return pltpu.make_async_remote_copy(
            src_ref=params_ref, dst_ref=pbuf.at[i], send_sem=psend.at[i], recv_sem=precv.at[i],
            device_id={"seg": target}, device_id_type=MESH)

    def send_params(i, o):
        @pl.when(exists(me - o))
        def _():
            params_copy(i, me - o).start()

    each(send_params)
    lax.fori_loop(0, pulse_count // ROWS, migrate_rows, 0)

    pulse = (me * pulse_count + lax.broadcasted_iota(jnp.int32, (ROWS, pulse_count), 1)).astype(jnp.float32)

    def term(packed):
        cols[...] = packed.T

        def weigh(q, carry):
            rows = pl.ds(pl.multiple_of(q * ROWS, ROWS), ROWS)
            low = pl.ds(pl.multiple_of(waves + q * ROWS, ROWS), ROWS)
            center, start, end = cols[rows, 0:1], cols[rows, 1:2], cols[rows, 2:3]
            rate, slope, amp = cols[rows, 3:4], cols[rows, 4:5], cols[rows, 5:6]
            r = (pulse - center) * scale
            t = r * (rate * r + slope)
            t = t - jnp.floor(t + 0.5)
            u = t * t
            s = t * horner(SIN, u)
            c = horner(COS, u)
            a = jnp.where((pulse >= start) & (pulse < end), amp, 0.0)
            twice = (a + a) * s
            wts[rows, :] = (a - twice * s).astype(jnp.bfloat16)
            wts[low, :] = (twice * c).astype(jnp.bfloat16)
            return carry

        lax.fori_loop(0, waves // ROWS, weigh, 0)
        real = jnp.dot(wts[...], mig[:, :gates], preferred_element_type=jnp.float32)
        imag = jnp.dot(wts[...], mig[:, gates:], preferred_element_type=jnp.float32)
        return real[:waves] - imag[waves:], imag[:waves] + real[waves:]

    def term_copy(i, target):
        return pltpu.make_async_remote_copy(
            src_ref=sendb.at[i], dst_ref=recvb.at[i], send_sem=tsend.at[i], recv_sem=trecv.at[i],
            device_id={"seg": target}, device_id_type=MESH)

    def send_term(i, o):
        @pl.when(exists(me + o))
        def _():
            params_copy(i, me + o).wait_recv()
            real, imag = term(pbuf[i])
            sendb[i, 0] = real.astype(jnp.bfloat16)
            sendb[i, 1] = imag.astype(jnp.bfloat16)
            term_copy(i, me + o).start()

    each(send_term)
    real, imag = term(params_ref[...])
    acc[0] = real
    acc[1] = imag

    def take(j, o):
        i = slots - 1 - j
        o = offset(i)

        @pl.when(exists(me - o))
        def _():
            term_copy(i, me - o).wait_recv()
            acc[0] += recvb[i, 0].astype(jnp.float32)
            acc[1] += recvb[i, 1].astype(jnp.float32)

    each(take)
    power[LOOK:LOOK + waves, :] = acc[0] * acc[0] + acc[1] * acc[1]

    def halo_copy(side):
        low = LOOK if side == 0 else waves
        into = LOOK + waves if side == 0 else 0
        target = me - 1 if side == 0 else me + 1
        return pltpu.make_async_remote_copy(
            src_ref=power.at[pl.ds(low, LOOK)], dst_ref=power.at[pl.ds(into, LOOK)],
            send_sem=hsend.at[side], recv_sem=hrecv.at[side],
            device_id={"seg": target}, device_id_type=MESH)

    @pl.when(me > 0)
    def _():
        halo_copy(0).start()

    @pl.when(me < n - 1)
    def _():
        halo_copy(1).start()

    @pl.when(me == 0)
    def _():
        power[0:LOOK, :] = jnp.zeros((LOOK, gates), jnp.float32)

    @pl.when(me == n - 1)
    def _():
        power[LOOK + waves:, :] = jnp.zeros((LOOK, gates), jnp.float32)

    focus_ref[...] = acc[...].astype(jnp.bfloat16)

    def drain(i, o):
        @pl.when(exists(me - o))
        def _():
            params_copy(i, me - o).wait_send()

        @pl.when(exists(me + o))
        def _():
            term_copy(i, me + o).wait_send()

    each(drain)

    @pl.when(me > 0)
    def _():
        halo_copy(0).wait_send()
        halo_copy(1).wait_recv()

    @pl.when(me < n - 1)
    def _():
        halo_copy(1).wait_send()
        halo_copy(0).wait_recv()

    total = power[...]
    size = waves + 2 * LOOK
    last = total[2 * LOOK:]
    step = 1
    while step < 2 * LOOK:
        size -= step
        total = total[:size] + total[step:step + size]
        step *= 2
    look_ref[...] = (total[:waves] + last) * (1.0 / float(2 * LOOK + 1))


def shards(pulses, fraction, gate_shift, aperture_start, aperture_end, doppler, chirp_rate):
    n = lax.axis_size("seg")
    pulse_count, gates = pulses.shape[1:]
    waves = aperture_start.shape[0]
    f32 = jnp.float32
    turn = 1.0 / (2.0 * math.pi)
    start, end = aperture_start, aperture_end
    none = jnp.zeros((waves,), f32)
    params = jnp.stack([
        ((start + end) // 2).astype(f32), start.astype(f32), end.astype(f32),
        chirp_rate * turn, doppler * turn, lax.rsqrt((end - start).astype(f32)), none, none])
    blank = jnp.zeros((pulse_count,), f32)
    packed = jnp.stack([fraction, gate_shift.astype(f32)] + [blank] * 6)
    vmem = pl.BlockSpec(memory_space=pltpu.VMEM)
    slots = 2 * REACH
    dma = pltpu.SemaphoreType.DMA
    return pl.pallas_call(
        functools.partial(kernel, n),
        out_shape=(jax.ShapeDtypeStruct((2, waves, gates), jnp.bfloat16),
                   jax.ShapeDtypeStruct((waves, gates), f32)),
        in_specs=[vmem] * 3,
        out_specs=(vmem, vmem),
        scratch_shapes=[
            pltpu.VMEM((pulse_count, 2 * gates), jnp.bfloat16),
            pltpu.VMEM((2 * waves, pulse_count), jnp.bfloat16),
            pltpu.VMEM((waves, 8), f32),
            pltpu.VMEM((pulse_count, 8), f32),
            pltpu.VMEM((slots, 8, waves), f32),
            pltpu.VMEM((slots, 2, waves, gates), jnp.bfloat16),
            pltpu.VMEM((slots, 2, waves, gates), jnp.bfloat16),
            pltpu.VMEM((2, waves, gates), f32),
            pltpu.VMEM((waves + 2 * LOOK, gates), f32),
            dma((slots,)), dma((slots,)), dma((slots,)), dma((slots,)), dma((2,)), dma((2,)),
        ],
        compiler_params=pltpu.CompilerParams(
            collective_id=0, has_side_effects=True, vmem_limit_bytes=16 * 1024 * 1024),
    )(pulses, packed, params)


def solution(mesh):
    seg = P(("arcs", "seg"))
    return jax.shard_map(
        shards,
        mesh=mesh,
        in_specs=(P(None, ("arcs", "seg"), None), seg, seg, seg, seg, seg, seg),
        out_specs=(P(None, ("arcs", "seg"), None), P(("arcs", "seg"), None)),
        check_vma=False,
    )
```

time: 67.3 us -> 30.2 us (0.45)
  starting transfers between devices: 30.5 us -> 0 us
  matrix products: 24.4 us -> 0 us
  Pallas kernels: 0 us -> 24 us
  other arithmetic: 5.89 us -> 0.09 us
  waiting for transfers between devices: 3.88 us -> 0 us
  local copies, waits for them, and re-layouts: 1.31 us -> 5.03 us
    ppermute x10 -> x0, starting transfers between devices: 30.5 us -> none  [the longest x8 22.5 us: from_behind(): return lax.ppermute(array, axis, pairs)]
    dot_general x36 -> x0, matrix products: 24.4 us -> none  [the longest x9 6.11 us: focus_block(): jnp.dot(weight_im, block_data[0], preferred_element_type=jnp.float32)]
    pallas_call x0 -> x1, Pallas kernels: none -> 24 us  [shards(): pl.pallas_call(functools.partial(kernel, n), out_shape=(jax.ShapeDtypeStr...]
    convert_element_type x6 -> x1, other arithmetic: 4.88 us -> 0.01 us  [shards(): packed = jnp.stack([fraction, gate_shift.astype(f32)] + [blank] * 6)]
    ppermute x10 -> x0, waiting for transfers between devices: 3.88 us -> none  [the longest x1 3.86 us: padded(): after = lax.ppermute(initial, axis, down)]
    unnamed x12 -> x16, local copies, waits for them, and re-layouts: 1.3 us -> 4.84 us
    div x1 -> x0, other arithmetic: 0.8 us -> none  [shards(): multilook = looked / float(2 * LOOK + 1)]
  transfers between devices with their start and end apart: 10 -> 0, of which waited for: 1 -> 0; matrix products, arithmetic and copies ran while one was open for 33% -> 0% of each run, Pallas kernels for 0% -> 0%
where the time goes in v1:
time: 30.2 us; the launch traced here: 29.8 us
  Pallas kernels  24 us (79%)
  local copies, waits for them, and re-layouts  5.03 us (17%)
  between operations  0.68 us (2%)
    pallas_call x1, Pallas kernels, shards(): pl.pallas_call(functools.partial(kernel, n), out_shape=(jax.ShapeDtypeStr...  24 us
    unnamed x16, local copies, waits for them, and re-layouts  4.84 us

profile of v1, /device:TPU:3, one launch (start us, length us, event | category | flops | bytes accessed | tf_op | source)
XLA Modules:
  0.0 29.8 jit_solution(17233357635504993994)
XLA Ops:
  0.6 0.0 copy-start.6
  0.6 0.6 %copy-done.6 = f32[128]{0:T(128)S(1)} copy-done((f32[128]{0:T(128)S(1)}, f32[128]{0:T(128)}, u32[]{:S(2)}) %copy-start.6) | copy-done | bytes 536
  1.3 0.1 pad.3.clone
  1.4 0.0 copy-start.3
  1.4 0.1 pad.2.clone
  1.4 0.6 %copy-done.3 = s32[256]{0:T(256)S(1)} copy-done((s32[256]{0:T(256)S(1)}, s32[256]{0:T(256)}, u32[]{:S(2)}) %copy-start.3) | copy-done | bytes 1048
  2.1 0.0 copy-start.1
  2.1 0.0 copy-start.2
  2.1 0.0 copy-start.5
  2.1 0.6 %copy-done.1 = s32[128]{0:T(128)S(1)} copy-done((s32[128]{0:T(128)S(1)}, s32[128]{0:T(128)}, u32[]{:S(2)}) %copy-start.1) | copy-done | bytes 536
  2.7 0.0 copy-done.2
  2.7 0.0 copy-done.5
  2.8 0.0 copy-start.4
  2.8 0.6 %copy-done.4 = f32[256]{0:T(256)S(1)} copy-done((f32[256]{0:T(256)S(1)}, f32[256]{0:T(256)}, u32[]{:S(2)}) %copy-start.4) | copy-done | bytes 1048
  3.5 0.1 maximum_maximum_fusion.gates_ref
  3.5 0.0 copy-start
  3.5 0.9 %copy-done = bf16[2,256,256]{2,1,0:T(8,128)(2,1)S(1)} copy-done((bf16[2,256,256]{2,1,0:T(8,128)(2,1)S(1)}, bf16[2,256,256]{2,1,0:T(8,128)(2,1)}, u32[]{:S(2)}) %copy-start) | copy-done | bytes 262168
  4.5 24.0 %shard_map.86 = (bf16[2,128,256]{2,1,0:T(8,128)(2,1)S(1)}, f32[128,256]{1,0:T(8,128)S(1)}) custom-call(bf16[2,256,256]{2,1,0:T(8,128)(2,1)S(1)} %copy-done, f32[8,256]{1,0:T(8,128)S(1)} %maximum_maximum_fusion.gates_ref, f32[8,128]{1,0:T(8,128)S(1)} %stack.51.params_ref), custom_call_target="tpu_custom_call" | custom-call | tf_op jit(solution)/shard_map/pallas_call | solution.py:224
  28.5 0.7 %copy.11 = bf16[2,128,256]{2,1,0:T(8,128)(2,1)} copy(bf16[2,128,256]{2,1,0:T(8,128)(2,1)S(1)} %get-tuple-element.9) | data formatting | bytes 262144
  29.1 0.7 %copy.12 = f32[128,256]{1,0:T(8,128)} copy(f32[128,256]{1,0:T(8,128)S(1)} %get-tuple-element.10) | data formatting | bytes 262144
  (8 shorter events, 0.1 us)
Async XLA Ops:
  0.6 0.7 %copy-start.6 = (f32[128]{0:T(128)S(1)}, f32[128]{0:T(128)}, u32[]{:S(2)}) copy-start(f32[128]{0:T(128)} %param.13) | copy-start | bytes 1540
  1.4 0.7 %copy-start.3 = (s32[256]{0:T(256)S(1)}, s32[256]{0:T(256)}, u32[]{:S(2)}) copy-start(s32[256]{0:T(256)} %param.9) | copy-start | bytes 3076
  2.1 0.7 %copy-start.1 = (s32[128]{0:T(128)S(1)}, s32[128]{0:T(128)}, u32[]{:S(2)}) copy-start(s32[128]{0:T(128)} %param.11) | copy-start | bytes 1540
  2.1 0.7 %copy-start.2 = (s32[128]{0:T(128)S(1)}, s32[128]{0:T(128)}, u32[]{:S(2)}) copy-start(s32[128]{0:T(128)} %param.10) | copy-start | bytes 1540
  2.1 0.7 %copy-start.5 = (f32[128]{0:T(128)S(1)}, f32[128]{0:T(128)}, u32[]{:S(2)}) copy-start(f32[128]{0:T(128)} %param.12) | copy-start | bytes 1540
  2.8 0.7 %copy-start.4 = (f32[256]{0:T(256)S(1)}, f32[256]{0:T(256)}, u32[]{:S(2)}) copy-start(f32[256]{0:T(256)} %param.8) | copy-start | bytes 3076
  3.5 0.9 %copy-start = (bf16[2,256,256]{2,1,0:T(8,128)(2,1)S(1)}, bf16[2,256,256]{2,1,0:T(8,128)(2,1)}, u32[]{:S(2)}) copy-start(bf16[2,256,256]{2,1,0:T(8,128)(2,1)} %pulses_ref.1) | copy-start | bytes 786436

commit v2 on v1

--- a/solution.py
+++ b/solution.py
@@ -25,36 +25,71 @@
     return result
 
 
-def kernel(n, pulses_ref, gates_ref, params_ref, focus_ref, look_ref,
-           mig, wts, cols, gcols, pbuf, sendb, recvb, acc, power,
-           psend, precv, tsend, trecv, hsend, hrecv):
+def kernel(n, pulses_hbm, fraction_hbm, shift_hbm, start_hbm, end_hbm, doppler_hbm, chirp_hbm,
+           focus_ref, look_ref,
+           pulses_ref, fraction_ref, shift_ref, start_ref, end_ref, doppler_ref, chirp_ref,
+           params_ref, gates_ref, mig, wts, cols, gcols, pbuf, helpb, gotb, sendb, recvb, acc, power,
+           insem, psend, precv, gsend, grecv, tsend, trecv, hsend, hrecv):
     me = lax.axis_index("seg")
+    core = lax.rem(me, 2)
+    way = 1 - 2 * core
+    mate = me + way
     pulse_count, gates = pulses_ref.shape[1:]
     waves = params_ref.shape[1]
     scale = 1.0 / float(REACH * pulse_count)
-    slots = 2 * REACH
-
-    def offset(i):
-        mag = REACH - lax.div(i, 2)
-        return mag * (1 - 2 * lax.rem(i, 2))
 
     def exists(d):
         return (d >= 0) & (d < n)
 
+    def loop(count, body):
+        def step(i, carry):
+            body(i)
+            return carry
+        lax.fori_loop(0, count, step, 0)
+
     def each(body):
-        def step(i, carry):
-            body(i, offset(i))
-            return carry
-        lax.fori_loop(0, slots, step, 0)
+        def peer(i):
+            @pl.when((i != REACH) & exists(me + i - REACH))
+            def _():
+                body(i, me + i - REACH)
+        loop(2 * REACH + 1, peer)
 
     barrier = pltpu.get_barrier_semaphore()
 
-    def greet(i, o):
-        @pl.when(exists(me + o))
-        def _():
-            pl.semaphore_signal(barrier, inc=1, device_id={"seg": me + o}, device_id_type=MESH)
+    def greet(i, peer):
+        pl.semaphore_signal(barrier, inc=1, device_id={"seg": peer}, device_id_type=MESH)
 
     each(greet)
+    loads = [pltpu.make_async_copy(src, dst, insem.at[i]) for i, (src, dst) in enumerate((
+        (start_hbm, start_ref), (end_hbm, end_ref), (doppler_hbm, doppler_ref), (chirp_hbm, chirp_ref),
+        (fraction_hbm, fraction_ref), (shift_hbm, shift_ref), (pulses_hbm, pulses_ref)))]
+    for load in loads:
+        load.start()
+    for load in loads[:4]:
+        load.wait()
+    start, end = start_ref[...], end_ref[...]
+    f32 = jnp.float32
+    turn = 1.0 / (2.0 * math.pi)
+    params_ref[0:1, :] = lax.shift_right_arithmetic(start + end, 1).astype(f32)
+    params_ref[1:2, :] = start.astype(f32)
+    params_ref[2:3, :] = end.astype(f32)
+    params_ref[3:4, :] = chirp_ref[...] * turn
+    params_ref[4:5, :] = doppler_ref[...] * turn
+    params_ref[5:6, :] = lax.rsqrt((end - start).astype(f32))
+    params_ref[6:8, :] = jnp.zeros((2, waves), f32)
+    pl.semaphore_wait(barrier, jnp.minimum(me, REACH) + jnp.minimum(n - 1 - me, REACH))
+
+    def params_copy(i, target):
+        return pltpu.make_async_remote_copy(
+            src_ref=params_ref, dst_ref=pbuf.at[i], send_sem=psend.at[i], recv_sem=precv.at[i],
+            device_id={"seg": target}, device_id_type=MESH)
+
+    each(lambda i, peer: params_copy(2 * REACH - i, peer).start())
+    for load in loads[4:]:
+        load.wait()
+    gates_ref[0:1, :] = fraction_ref[...]
+    gates_ref[1:2, :] = shift_ref[...].astype(f32)
+    gates_ref[2:8, :] = jnp.zeros((6, pulse_count), f32)
     gcols[...] = gates_ref[...].T
     lane = lax.broadcasted_iota(jnp.int32, (ROWS, gates), 1)
 
@@ -72,19 +107,6 @@
             mig[rows, c * gates:(c + 1) * gates] = z.astype(jnp.bfloat16)
         return carry
 
-    pl.semaphore_wait(barrier, jnp.minimum(me, REACH) + jnp.minimum(n - 1 - me, REACH))
-
-    def params_copy(i, target):
-        return pltpu.make_async_remote_copy(
-            src_ref=params_ref, dst_ref=pbuf.at[i], send_sem=psend.at[i], recv_sem=precv.at[i],
-            device_id={"seg": target}, device_id_type=MESH)
-
-    def send_params(i, o):
-        @pl.when(exists(me - o))
-        def _():
-            params_copy(i, me - o).start()
-
-    each(send_params)
     lax.fori_loop(0, pulse_count // ROWS, migrate_rows, 0)
 
     pulse = (me * pulse_count + lax.broadcasted_iota(jnp.int32, (ROWS, pulse_count), 1)).astype(jnp.float32)
@@ -114,36 +136,73 @@
         imag = jnp.dot(wts[...], mig[:, gates:], preferred_element_type=jnp.float32)
         return real[:waves] - imag[waves:], imag[:waves] + real[waves:]
 
-    def term_copy(i, target):
+    def term_for(o):
+        i = o + REACH
+        params_copy(i, me + o).wait_recv()
+        return term(pbuf[i])
+
+    def own(k):
+        return 4 - 2 * k - 2 * lax.div(k, 2)
+
+    def help_copy(k):
         return pltpu.make_async_remote_copy(
-            src_ref=sendb.at[i], dst_ref=recvb.at[i], send_sem=tsend.at[i], recv_sem=trecv.at[i],
+            src_ref=helpb.at[k], dst_ref=gotb.at[k], send_sem=gsend.at[k], recv_sem=grecv.at[k],
+            device_id={"seg": mate}, device_id_type=MESH)
+
+    def sum_copy(k, target):
+        return pltpu.make_async_remote_copy(
+            src_ref=sendb.at[k], dst_ref=recvb.at[k], send_sem=tsend.at[k], recv_sem=trecv.at[k],
             device_id={"seg": target}, device_id_type=MESH)
 
-    def send_term(i, o):
+    def alone(k):
+        @pl.when(exists(me + way * own(k)))
+        def _():
+            real, imag = term_for(way * own(k))
+            sendb[k, 0] = real.astype(jnp.bfloat16)
+            sendb[k, 1] = imag.astype(jnp.bfloat16)
+            sum_copy(k, me + way * own(k)).start()
+
+    def assist(k):
+        o = way * (1 - own(k))
+
         @pl.when(exists(me + o))
         def _():
-            params_copy(i, me + o).wait_recv()
-            real, imag = term(pbuf[i])
-            sendb[i, 0] = real.astype(jnp.bfloat16)
-            sendb[i, 1] = imag.astype(jnp.bfloat16)
-            term_copy(i, me + o).start()
-
-    each(send_term)
+            real, imag = term_for(o)
+            helpb[k, 0] = real.astype(jnp.bfloat16)
+            helpb[k, 1] = imag.astype(jnp.bfloat16)
+            help_copy(k).start()
+
+    def shared(k):
+        @pl.when(exists(me + way * own(k)))
+        def _():
+            real, imag = term_for(way * own(k))
+            help_copy(k).wait_recv()
+            sendb[k, 0] = (real + gotb[k, 0].astype(f32)).astype(jnp.bfloat16)
+            sendb[k, 1] = (imag + gotb[k, 1].astype(f32)).astype(jnp.bfloat16)
+            sum_copy(k, me + way * own(k)).start()
+
+    loop(1, lambda k: alone(k + 3))
+    loop(3, assist)
+    loop(3, shared)
+    real, imag = term_for(way)
+    helpb[3, 0] = real.astype(jnp.bfloat16)
+    helpb[3, 1] = imag.astype(jnp.bfloat16)
+    help_copy(3).start()
     real, imag = term(params_ref[...])
-    acc[0] = real
-    acc[1] = imag
-
-    def take(j, o):
-        i = slots - 1 - j
-        o = offset(i)
-
-        @pl.when(exists(me - o))
-        def _():
-            term_copy(i, me - o).wait_recv()
-            acc[0] += recvb[i, 0].astype(jnp.float32)
-            acc[1] += recvb[i, 1].astype(jnp.float32)
-
-    each(take)
+    help_copy(3).wait_recv()
+    acc[0] = real + gotb[3, 0].astype(f32)
+    acc[1] = imag + gotb[3, 1].astype(f32)
+
+    def take(j):
+        k = 3 - j
+
+        @pl.when(exists(me - way * own(k)))
+        def _():
+            sum_copy(k, me - way * own(k)).wait_recv()
+            acc[0] += recvb[k, 0].astype(f32)
+            acc[1] += recvb[k, 1].astype(f32)
+
+    loop(4, take)
     power[LOOK:LOOK + waves, :] = acc[0] * acc[0] + acc[1] * acc[1]
 
     def halo_copy(side):
@@ -173,16 +232,22 @@
 
     focus_ref[...] = acc[...].astype(jnp.bfloat16)
 
-    def drain(i, o):
-        @pl.when(exists(me - o))
-        def _():
-            params_copy(i, me - o).wait_send()
-
-        @pl.when(exists(me + o))
-        def _():
-            term_copy(i, me + o).wait_send()
-
-    each(drain)
+    each(lambda i, peer: params_copy(2 * REACH - i, peer).wait_send())
+
+    def drain(k):
+        @pl.when(exists(me + way * own(k)))
+        def _():
+            sum_copy(k, me + way * own(k)).wait_send()
+
+    loop(4, drain)
+
+    def drain_help(k):
+        @pl.when(exists(me + way * (1 - own(k))))
+        def _():
+            help_copy(k).wait_send()
+
+    loop(3, drain_help)
+    help_copy(3).wait_send()
 
     @pl.when(me > 0)
     def _():
@@ -210,38 +275,35 @@
     pulse_count, gates = pulses.shape[1:]
     waves = aperture_start.shape[0]
     f32 = jnp.float32
-    turn = 1.0 / (2.0 * math.pi)
-    start, end = aperture_start, aperture_end
-    none = jnp.zeros((waves,), f32)
-    params = jnp.stack([
-        ((start + end) // 2).astype(f32), start.astype(f32), end.astype(f32),
-        chirp_rate * turn, doppler * turn, lax.rsqrt((end - start).astype(f32)), none, none])
-    blank = jnp.zeros((pulse_count,), f32)
-    packed = jnp.stack([fraction, gate_shift.astype(f32)] + [blank] * 6)
     vmem = pl.BlockSpec(memory_space=pltpu.VMEM)
-    slots = 2 * REACH
+    hbm = pl.BlockSpec(memory_space=pltpu.HBM)
+    slots = 2 * REACH + 1
     dma = pltpu.SemaphoreType.DMA
+    block = pltpu.VMEM((4, 2, waves, gates), jnp.bfloat16)
+    rows = [a.reshape(1, -1) for a in (
+        fraction, gate_shift, aperture_start, aperture_end, doppler, chirp_rate)]
     return pl.pallas_call(
         functools.partial(kernel, n),
         out_shape=(jax.ShapeDtypeStruct((2, waves, gates), jnp.bfloat16),
                    jax.ShapeDtypeStruct((waves, gates), f32)),
-        in_specs=[vmem] * 3,
+        in_specs=[hbm] * 7,
         out_specs=(vmem, vmem),
-        scratch_shapes=[
+        scratch_shapes=[pltpu.VMEM(pulses.shape, pulses.dtype)] + [pltpu.VMEM(a.shape, a.dtype) for a in rows] + [
+            pltpu.VMEM((8, waves), f32),
+            pltpu.VMEM((8, pulse_count), f32),
             pltpu.VMEM((pulse_count, 2 * gates), jnp.bfloat16),
             pltpu.VMEM((2 * waves, pulse_count), jnp.bfloat16),
             pltpu.VMEM((waves, 8), f32),
             pltpu.VMEM((pulse_count, 8), f32),
             pltpu.VMEM((slots, 8, waves), f32),
-            pltpu.VMEM((slots, 2, waves, gates), jnp.bfloat16),
-            pltpu.VMEM((slots, 2, waves, gates), jnp.bfloat16),
+            block, block, block, block,
             pltpu.VMEM((2, waves, gates), f32),
             pltpu.VMEM((waves + 2 * LOOK, gates), f32),
-            dma((slots,)), dma((slots,)), dma((slots,)), dma((slots,)), dma((2,)), dma((2,)),
+            dma((7,)), dma((slots,)), dma((slots,)), dma((4,)), dma((4,)), dma((4,)), dma((4,)), dma((2,)), dma((2,)),
         ],
         compiler_params=pltpu.CompilerParams(
-            collective_id=0, has_side_effects=True, vmem_limit_bytes=16 * 1024 * 1024),
-    )(pulses, packed, params)
+            collective_id=0, has_side_effects=True, vmem_limit_bytes=60 * 1024 * 1024),
+    )(pulses, *rows)
 
 
 def solution(mesh):

time: 30.2 us -> 25.4 us (0.84)
  the two profiles are of different devices: /device:TPU:3 before, /device:TPU:11 now
where the time goes in v2:
time: 25.4 us; the launch traced here: 25.2 us
  Pallas kernels  22.3 us (88%)
  local copies, waits for them, and re-layouts  2.26 us (9%)
  between operations  0.65 us (3%)
    pallas_call x1, Pallas kernels, shards(): pl.pallas_call(functools.partial(kernel, n), out_shape=(jax.ShapeDtypeStr...  22.3 us
    unnamed x4, local copies, waits for them, and re-layouts  2.26 us

profile of v2, /device:TPU:11, one launch (start us, length us, event | category | flops | bytes accessed | tf_op | source)
XLA Modules:
  0.0 25.2 jit_solution(5164811759417292843)
XLA Ops:
  0.6 22.3 %shard_map.86 = (bf16[2,128,256]{2,1,0:T(8,128)(2,1)}, f32[128,256]{1,0:T(8,128)}) custom-call(bf16[2,256,256]{2,1,0:T(8,128)(2,1)} %pulses_hbm.1, f32[1,256]{1,0:T(1,128)} %bitcast.6, s32[1,256]{1,0:T(1,128)} %bitcast.7, s32[1,128]{1,0:T(1,128)} %bitcast.8, s32[1,128]{1,0:T(1,128)} %bitcast.9, f32[1,128]{1,0:T(1,128)} %bitcast.10, f32[1,128]{1,0:T(1,128)} %bitcast.11), custom_call_target="tpu_custom_call" | custom-call | tf_op jit(solution)/shard_map/pallas_call | solution.py:285
  22.9 0.0 copy-start
  23.0 1.6 %copy.11 = bf16[2,128,256]{2,1,0:T(8,128)(2,1)} copy(bf16[2,128,256]{2,1,0:T(8,128)(2,1)} %get-tuple-element.4) | data formatting | bytes 262144
  24.6 0.0 copy-done
  24.6 0.7 %copy.12 = f32[128,256]{1,0:T(8,128)} copy(f32[128,256]{1,0:T(8,128)S(1)} %copy-done) | data formatting | bytes 262144
Async XLA Ops:
  22.9 1.6 %copy-start = (f32[128,256]{1,0:T(8,128)S(1)}, f32[128,256]{1,0:T(8,128)}, u32[]{:S(2)}) copy-start(f32[128,256]{1,0:T(8,128)} %get-tuple-element.5) | copy-start | bytes 393220

commit v3 on v2

--- a/solution.py
+++ b/solution.py
@@ -107,7 +107,7 @@
             mig[rows, c * gates:(c + 1) * gates] = z.astype(jnp.bfloat16)
         return carry
 
-    lax.fori_loop(0, pulse_count // ROWS, migrate_rows, 0)
+    lax.fori_loop(0, pulse_count // ROWS, migrate_rows, 0, unroll=4)
 
     pulse = (me * pulse_count + lax.broadcasted_iota(jnp.int32, (ROWS, pulse_count), 1)).astype(jnp.float32)
 
@@ -131,7 +131,7 @@
             wts[low, :] = (twice * c).astype(jnp.bfloat16)
             return carry
 
-        lax.fori_loop(0, waves // ROWS, weigh, 0)
+        lax.fori_loop(0, waves // ROWS, weigh, 0, unroll=True)
         real = jnp.dot(wts[...], mig[:, :gates], preferred_element_type=jnp.float32)
         imag = jnp.dot(wts[...], mig[:, gates:], preferred_element_type=jnp.float32)
         return real[:waves] - imag[waves:], imag[:waves] + real[waves:]
@@ -232,6 +232,18 @@
 
     focus_ref[...] = acc[...].astype(jnp.bfloat16)
 
+    def average(low, count):
+        size = count + 2 * LOOK
+        total = power[low:low + size, :]
+        last = total[2 * LOOK:]
+        step = 1
+        while step < 2 * LOOK:
+            size -= step
+            total = total[:size] + total[step:step + size]
+            step *= 2
+        look_ref[low:low + count, :] = (total[:count] + last) * (1.0 / float(2 * LOOK + 1))
+
+    average(LOOK, waves - 2 * LOOK)
     each(lambda i, peer: params_copy(2 * REACH - i, peer).wait_send())
 
     def drain(k):
@@ -259,15 +271,8 @@
         halo_copy(1).wait_send()
         halo_copy(0).wait_recv()
 
-    total = power[...]
-    size = waves + 2 * LOOK
-    last = total[2 * LOOK:]
-    step = 1
-    while step < 2 * LOOK:
-        size -= step
-        total = total[:size] + total[step:step + size]
-        step *= 2
-    look_ref[...] = (total[:waves] + last) * (1.0 / float(2 * LOOK + 1))
+    average(0, LOOK)
+    average(waves - LOOK, LOOK)
 
 
 def shards(pulses, fraction, gate_shift, aperture_start, aperture_end, doppler, chirp_rate):

time: 25.4 us -> 22.9 us (0.902)
  the two profiles are of different devices: /device:TPU:11 before, /device:TPU:3 now
where the time goes in v3:
time: 22.9 us; the launch traced here: 22.7 us
  Pallas kernels  19.8 us (86%)
  local copies, waits for them, and re-layouts  2.26 us (10%)
  between operations  0.65 us (3%)
    pallas_call x1, Pallas kernels, shards(): pl.pallas_call(functools.partial(kernel, n), out_shape=(jax.ShapeDtypeStr...  19.8 us
    unnamed x4, local copies, waits for them, and re-layouts  2.26 us

profile of v3, /device:TPU:3, one launch (start us, length us, event | category | flops | bytes accessed | tf_op | source)
XLA Modules:
  0.0 22.7 jit_solution(3820572995106912529)
XLA Ops:
  0.6 19.8 %shard_map.86 = (bf16[2,128,256]{2,1,0:T(8,128)(2,1)}, f32[128,256]{1,0:T(8,128)}) custom-call(bf16[2,256,256]{2,1,0:T(8,128)(2,1)} %pulses_hbm.1, f32[1,256]{1,0:T(1,128)} %bitcast.6, s32[1,256]{1,0:T(1,128)} %bitcast.7, s32[1,128]{1,0:T(1,128)} %bitcast.8, s32[1,128]{1,0:T(1,128)} %bitcast.9, f32[1,128]{1,0:T(1,128)} %bitcast.10, f32[1,128]{1,0:T(1,128)} %bitcast.11), custom_call_target="tpu_custom_call" | custom-call | tf_op jit(solution)/shard_map/pallas_call | solution.py:290
  20.5 0.0 copy-start
  20.5 1.6 %copy.11 = bf16[2,128,256]{2,1,0:T(8,128)(2,1)} copy(bf16[2,128,256]{2,1,0:T(8,128)(2,1)} %get-tuple-element.4) | data formatting | bytes 262144
  22.1 0.0 copy-done
  22.1 0.7 %copy.12 = f32[128,256]{1,0:T(8,128)} copy(f32[128,256]{1,0:T(8,128)S(1)} %copy-done) | data formatting | bytes 262144
Async XLA Ops:
  20.5 1.6 %copy-start = (f32[128,256]{1,0:T(8,128)S(1)}, f32[128,256]{1,0:T(8,128)}, u32[]{:S(2)}) copy-start(f32[128,256]{1,0:T(8,128)} %get-tuple-element.5) | copy-start | bytes 393220

commit v4 on v3

--- a/solution.py
+++ b/solution.py
@@ -26,10 +26,10 @@
 
 
 def kernel(n, pulses_hbm, fraction_hbm, shift_hbm, start_hbm, end_hbm, doppler_hbm, chirp_hbm,
-           focus_ref, look_ref,
+           focus_hbm, look_hbm, focus_ref, look_ref,
            pulses_ref, fraction_ref, shift_ref, start_ref, end_ref, doppler_ref, chirp_ref,
            params_ref, gates_ref, mig, wts, cols, gcols, pbuf, helpb, gotb, sendb, recvb, acc, power,
-           insem, psend, precv, gsend, grecv, tsend, trecv, hsend, hrecv):
+           outsem, insem, psend, precv, gsend, grecv, tsend, trecv, hsend, hrecv):
     me = lax.axis_index("seg")
     core = lax.rem(me, 2)
     way = 1 - 2 * core
@@ -77,14 +77,11 @@
     params_ref[4:5, :] = doppler_ref[...] * turn
     params_ref[5:6, :] = lax.rsqrt((end - start).astype(f32))
     params_ref[6:8, :] = jnp.zeros((2, waves), f32)
-    pl.semaphore_wait(barrier, jnp.minimum(me, REACH) + jnp.minimum(n - 1 - me, REACH))
-
     def params_copy(i, target):
         return pltpu.make_async_remote_copy(
             src_ref=params_ref, dst_ref=pbuf.at[i], send_sem=psend.at[i], recv_sem=precv.at[i],
             device_id={"seg": target}, device_id_type=MESH)
 
-    each(lambda i, peer: params_copy(2 * REACH - i, peer).start())
     for load in loads[4:]:
         load.wait()
     gates_ref[0:1, :] = fraction_ref[...]
@@ -107,7 +104,11 @@
             mig[rows, c * gates:(c + 1) * gates] = z.astype(jnp.bfloat16)
         return carry
 
-    lax.fori_loop(0, pulse_count // ROWS, migrate_rows, 0, unroll=4)
+    chunks = pulse_count // ROWS
+    lax.fori_loop(0, chunks // 2, migrate_rows, 0, unroll=4)
+    pl.semaphore_wait(barrier, jnp.minimum(me, REACH) + jnp.minimum(n - 1 - me, REACH))
+    each(lambda i, peer: params_copy(2 * REACH - i, peer).start())
+    lax.fori_loop(chunks // 2, chunks, migrate_rows, 0, unroll=4)
 
     pulse = (me * pulse_count + lax.broadcasted_iota(jnp.int32, (ROWS, pulse_count), 1)).astype(jnp.float32)
 
@@ -142,7 +143,7 @@
         return term(pbuf[i])
 
     def own(k):
-        return 4 - 2 * k - 2 * lax.div(k, 2)
+        return 4 - 2 * k - 2 * (k // 2)
 
     def help_copy(k):
         return pltpu.make_async_remote_copy(
@@ -181,17 +182,21 @@
             sendb[k, 1] = (imag + gotb[k, 1].astype(f32)).astype(jnp.bfloat16)
             sum_copy(k, me + way * own(k)).start()
 
-    loop(1, lambda k: alone(k + 3))
-    loop(3, assist)
-    loop(3, shared)
+    acc[0], acc[1] = term(params_ref[...])
+    alone(3)
+    assist(0)
+    assist(1)
+    shared(0)
+    assist(2)
+    shared(1)
+    shared(2)
     real, imag = term_for(way)
     helpb[3, 0] = real.astype(jnp.bfloat16)
     helpb[3, 1] = imag.astype(jnp.bfloat16)
     help_copy(3).start()
-    real, imag = term(params_ref[...])
     help_copy(3).wait_recv()
-    acc[0] = real + gotb[3, 0].astype(f32)
-    acc[1] = imag + gotb[3, 1].astype(f32)
+    acc[0] += gotb[3, 0].astype(f32)
+    acc[1] += gotb[3, 1].astype(f32)
 
     def take(j):
         k = 3 - j
@@ -231,6 +236,9 @@
         power[LOOK + waves:, :] = jnp.zeros((LOOK, gates), jnp.float32)
 
     focus_ref[...] = acc[...].astype(jnp.bfloat16)
+    focus_out = pltpu.make_async_copy(focus_ref, focus_hbm, outsem.at[0])
+    look_out = pltpu.make_async_copy(look_ref, look_hbm, outsem.at[1])
+    focus_out.start()
 
     def average(low, count):
         size = count + 2 * LOOK
@@ -273,6 +281,18 @@
 
     average(0, LOOK)
     average(waves - LOOK, LOOK)
+    look_out.start()
+    focus_out.wait()
+    look_out.wait()
+
+
+def hand_over(focus_in, look_in, focus_out, look_out, sems):
+    copies = [pltpu.make_async_copy(focus_in, focus_out, sems.at[0]),
+              pltpu.make_async_copy(look_in, look_out, sems.at[1])]
+    for copy in copies:
+        copy.start()
+    for copy in copies:
+        copy.wait()
 
 
 def shards(pulses, fraction, gate_shift, aperture_start, aperture_end, doppler, chirp_rate):
@@ -280,20 +300,19 @@
     pulse_count, gates = pulses.shape[1:]
     waves = aperture_start.shape[0]
     f32 = jnp.float32
-    vmem = pl.BlockSpec(memory_space=pltpu.VMEM)
     hbm = pl.BlockSpec(memory_space=pltpu.HBM)
     slots = 2 * REACH + 1
     dma = pltpu.SemaphoreType.DMA
     block = pltpu.VMEM((4, 2, waves, gates), jnp.bfloat16)
     rows = [a.reshape(1, -1) for a in (
         fraction, gate_shift, aperture_start, aperture_end, doppler, chirp_rate)]
-    return pl.pallas_call(
+    outs = (jax.ShapeDtypeStruct((2, waves, gates), jnp.bfloat16), jax.ShapeDtypeStruct((waves, gates), f32))
+    results = pl.pallas_call(
         functools.partial(kernel, n),
-        out_shape=(jax.ShapeDtypeStruct((2, waves, gates), jnp.bfloat16),
-                   jax.ShapeDtypeStruct((waves, gates), f32)),
+        out_shape=outs,
         in_specs=[hbm] * 7,
-        out_specs=(vmem, vmem),
-        scratch_shapes=[pltpu.VMEM(pulses.shape, pulses.dtype)] + [pltpu.VMEM(a.shape, a.dtype) for a in rows] + [
+        out_specs=(hbm, hbm),
+        scratch_shapes=[pltpu.VMEM(o.shape, o.dtype) for o in outs] + [pltpu.VMEM(pulses.shape, pulses.dtype)] + [pltpu.VMEM(a.shape, a.dtype) for a in rows] + [
             pltpu.VMEM((8, waves), f32),
             pltpu.VMEM((8, pulse_count), f32),
             pltpu.VMEM((pulse_count, 2 * gates), jnp.bfloat16),
@@ -304,11 +323,14 @@
             block, block, block, block,
             pltpu.VMEM((2, waves, gates), f32),
             pltpu.VMEM((waves + 2 * LOOK, gates), f32),
-            dma((7,)), dma((slots,)), dma((slots,)), dma((4,)), dma((4,)), dma((4,)), dma((4,)), dma((2,)), dma((2,)),
+            dma((2,)), dma((7,)), dma((slots,)), dma((slots,)), dma((4,)), dma((4,)), dma((4,)), dma((4,)), dma((2,)), dma((2,)),
         ],
         compiler_params=pltpu.CompilerParams(
             collective_id=0, has_side_effects=True, vmem_limit_bytes=60 * 1024 * 1024),
     )(pulses, *rows)
+    return pl.pallas_call(
+        hand_over, out_shape=outs, in_specs=[hbm, hbm], out_specs=(hbm, hbm), scratch_shapes=[dma((2,))],
+    )(*results)
 
 
 def solution(mesh):

time: 22.9 us -> 30.3 us (1.32)
  Pallas kernels: 19.8 us -> 29.5 us
  local copies, waits for them, and re-layouts: 2.26 us -> 0 us
    pallas_call x1 -> x2, Pallas kernels: 19.8 us -> 29.5 us  [the longest x1 20.4 us: shards(): pl.pallas_call(functools.partial(kernel, n), out_shape=outs, in_specs=[hb...]
    unnamed x4 -> x0, local copies, waits for them, and re-layouts: 2.26 us -> none
where the time goes in v4:
time: 30.3 us; the launch traced here: 30.1 us
  Pallas kernels  29.5 us (97%)
  between operations  0.64 us (2%)
    pallas_call x1, Pallas kernels, shards(): pl.pallas_call(functools.partial(kernel, n), out_shape=outs, in_specs=[hb...  20.4 us
    pallas_call x1, Pallas kernels, shards(): pl.pallas_call(hand_over, out_shape=outs, in_specs=[hbm, hbm], out_specs=...  9.06 us

profile of v4, /device:TPU:3, one launch (start us, length us, event | category | flops | bytes accessed | tf_op | source)
XLA Modules:
  0.0 30.1 jit_solution(7041405929567861159)
XLA Ops:
  0.6 20.4 %shard_map.86 = (bf16[2,128,256]{2,1,0:T(8,128)(2,1)}, f32[128,256]{1,0:T(8,128)}) custom-call(bf16[2,256,256]{2,1,0:T(8,128)(2,1)} %pulses_hbm.1, f32[1,256]{1,0:T(1,128)} %bitcast.6, s32[1,256]{1,0:T(1,128)} %bitcast.7, s32[1,128]{1,0:T(1,128)} %bitcast.8, s32[1,128]{1,0:T(1,128)} %bitcast.9, f32[1,128]{1,0:T(1,128)} %bitcast.10, f32[1,128]{1,0:T(1,128)} %bitcast.11), custom_call_target="tpu_custom_call" | custom-call | tf_op jit(solution)/shard_map/pallas_call | solution.py:310
  21.0 9.1 %shard_map.87 = (bf16[2,128,256]{2,1,0:T(8,128)(2,1)}, f32[128,256]{1,0:T(8,128)}) custom-call(bf16[2,128,256]{2,1,0:T(8,128)(2,1)} %get-tuple-element.4.focus_in, f32[128,256]{1,0:T(8,128)} %get-tuple-element.5.look_in), custom_call_target="tpu_custom_call" | custom-call | tf_op jit(solution)/shard_map/pallas_call | solution.py:331

commit v5 on v3

--- a/solution.py
+++ b/solution.py
@@ -275,6 +275,19 @@
     average(waves - LOOK, LOOK)
 
 
+def hand_over(focus_in, look_in, focus_out, look_out, focus, look, sems):
+    arrays = ((focus_in, focus, focus_out), (look_in, look, look_out))
+    loads = [pltpu.make_async_copy(a, b, sems.at[i]) for i, (a, b, _) in enumerate(arrays)]
+    stores = [pltpu.make_async_copy(b, c, sems.at[2 + i]) for i, (_, b, c) in enumerate(arrays)]
+    for load in loads:
+        load.start()
+    for load, store in zip(loads, stores):
+        load.wait()
+        store.start()
+    for store in stores:
+        store.wait()
+
+
 def shards(pulses, fraction, gate_shift, aperture_start, aperture_end, doppler, chirp_rate):
     n = lax.axis_size("seg")
     pulse_count, gates = pulses.shape[1:]
@@ -287,10 +300,10 @@
     block = pltpu.VMEM((4, 2, waves, gates), jnp.bfloat16)
     rows = [a.reshape(1, -1) for a in (
         fraction, gate_shift, aperture_start, aperture_end, doppler, chirp_rate)]
-    return pl.pallas_call(
+    outs = (jax.ShapeDtypeStruct((2, waves, gates), jnp.bfloat16), jax.ShapeDtypeStruct((waves, gates), f32))
+    results = pl.pallas_call(
         functools.partial(kernel, n),
-        out_shape=(jax.ShapeDtypeStruct((2, waves, gates), jnp.bfloat16),
-                   jax.ShapeDtypeStruct((waves, gates), f32)),
+        out_shape=outs,
         in_specs=[hbm] * 7,
         out_specs=(vmem, vmem),
         scratch_shapes=[pltpu.VMEM(pulses.shape, pulses.dtype)] + [pltpu.VMEM(a.shape, a.dtype) for a in rows] + [
@@ -309,6 +322,11 @@
         compiler_params=pltpu.CompilerParams(
             collective_id=0, has_side_effects=True, vmem_limit_bytes=60 * 1024 * 1024),
     )(pulses, *rows)
+    return pl.pallas_call(
+        hand_over, out_shape=outs, in_specs=[hbm, hbm], out_specs=(hbm, hbm),
+        scratch_shapes=[pltpu.VMEM(o.shape, o.dtype) for o in outs] + [dma((4,))],
+        compiler_params=pltpu.CompilerParams(vmem_limit_bytes=60 * 1024 * 1024),
+    )(*results)
 
 
 def solution(mesh):

time: 22.9 us -> 22.3 us (0.974)
  local copies, waits for them, and re-layouts: 2.26 us -> 0 us
  Pallas kernels: 19.8 us -> 21.5 us
    unnamed x4 -> x0, local copies, waits for them, and re-layouts: 2.26 us -> none
    pallas_call x1 -> x2, Pallas kernels: 19.8 us -> 21.5 us  [the longest x1 19.8 us: shards(): pl.pallas_call(functools.partial(kernel, n), out_shape=outs, in_specs=[hb...]
where the time goes in v5:
time: 22.3 us; the launch traced here: 22.1 us
  Pallas kernels  21.5 us (96%)
  between operations  0.64 us (3%)
    pallas_call x1, Pallas kernels, shards(): pl.pallas_call(functools.partial(kernel, n), out_shape=outs, in_specs=[hb...  19.8 us
    pallas_call x1, Pallas kernels, shards(): pl.pallas_call(hand_over, out_shape=outs, in_specs=[hbm, hbm], out_specs=...  1.66 us

profile of v5, /device:TPU:3, one launch (start us, length us, event | category | flops | bytes accessed | tf_op | source)
XLA Modules:
  0.0 22.1 jit_solution(17743216373162116911)
XLA Ops:
  0.6 19.8 %shard_map.86 = (bf16[2,128,256]{2,1,0:T(8,128)(2,1)}, f32[128,256]{1,0:T(8,128)}) custom-call(bf16[2,256,256]{2,1,0:T(8,128)(2,1)} %pulses_hbm.1, f32[1,256]{1,0:T(1,128)} %bitcast.6, s32[1,256]{1,0:T(1,128)} %bitcast.7, s32[1,128]{1,0:T(1,128)} %bitcast.8, s32[1,128]{1,0:T(1,128)} %bitcast.9, f32[1,128]{1,0:T(1,128)} %bitcast.10, f32[1,128]{1,0:T(1,128)} %bitcast.11), custom_call_target="tpu_custom_call" | custom-call | tf_op jit(solution)/shard_map/pallas_call | solution.py:304
  20.5 1.7 %shard_map.87 = (bf16[2,128,256]{2,1,0:T(8,128)(2,1)}, f32[128,256]{1,0:T(8,128)}) custom-call(bf16[2,128,256]{2,1,0:T(8,128)(2,1)} %get-tuple-element.4.focus_in, f32[128,256]{1,0:T(8,128)} %get-tuple-element.5.look_in), custom_call_target="tpu_custom_call" | custom-call | tf_op jit(solution)/shard_map/pallas_call | solution.py:325

commit v6 on v5

--- a/solution.py
+++ b/solution.py
@@ -182,8 +182,10 @@
             sum_copy(k, me + way * own(k)).start()
 
     loop(1, lambda k: alone(k + 3))
-    loop(3, assist)
-    loop(3, shared)
+    loop(2, assist)
+    loop(1, shared)
+    loop(1, lambda k: assist(k + 2))
+    loop(2, lambda k: shared(k + 1))
     real, imag = term_for(way)
     helpb[3, 0] = real.astype(jnp.bfloat16)
     helpb[3, 1] = imag.astype(jnp.bfloat16)

time: 22.3 us -> 22.4 us (level)
  no operation moved by 1% of the time
where the time goes in v6:
time: 22.4 us; the launch traced here: 22.2 us
  Pallas kernels  21.5 us (96%)
  between operations  0.64 us (3%)
    pallas_call x1, Pallas kernels, shards(): pl.pallas_call(functools.partial(kernel, n), out_shape=outs, in_specs=[hb...  19.9 us
    pallas_call x1, Pallas kernels, shards(): pl.pallas_call(hand_over, out_shape=outs, in_specs=[hbm, hbm], out_specs=...  1.66 us

profile of v6, /device:TPU:3, one launch (start us, length us, event | category | flops | bytes accessed | tf_op | source)
XLA Modules:
  0.0 22.2 jit_solution(6108974363426842904)
XLA Ops:
  0.6 19.9 %shard_map.86 = (bf16[2,128,256]{2,1,0:T(8,128)(2,1)}, f32[128,256]{1,0:T(8,128)}) custom-call(bf16[2,256,256]{2,1,0:T(8,128)(2,1)} %pulses_hbm.1, f32[1,256]{1,0:T(1,128)} %bitcast.6, s32[1,256]{1,0:T(1,128)} %bitcast.7, s32[1,128]{1,0:T(1,128)} %bitcast.8, s32[1,128]{1,0:T(1,128)} %bitcast.9, f32[1,128]{1,0:T(1,128)} %bitcast.10, f32[1,128]{1,0:T(1,128)} %bitcast.11), custom_call_target="tpu_custom_call" | custom-call | tf_op jit(solution)/shard_map/pallas_call | solution.py:306
  20.5 1.7 %shard_map.87 = (bf16[2,128,256]{2,1,0:T(8,128)(2,1)}, f32[128,256]{1,0:T(8,128)}) custom-call(bf16[2,128,256]{2,1,0:T(8,128)(2,1)} %get-tuple-element.4.focus_in, f32[128,256]{1,0:T(8,128)} %get-tuple-element.5.look_in), custom_call_target="tpu_custom_call" | custom-call | tf_op jit(solution)/shard_map/pallas_call | solution.py:327

commit v7 on v5

--- a/solution.py
+++ b/solution.py
@@ -77,14 +77,11 @@
     params_ref[4:5, :] = doppler_ref[...] * turn
     params_ref[5:6, :] = lax.rsqrt((end - start).astype(f32))
     params_ref[6:8, :] = jnp.zeros((2, waves), f32)
-    pl.semaphore_wait(barrier, jnp.minimum(me, REACH) + jnp.minimum(n - 1 - me, REACH))
-
     def params_copy(i, target):
         return pltpu.make_async_remote_copy(
             src_ref=params_ref, dst_ref=pbuf.at[i], send_sem=psend.at[i], recv_sem=precv.at[i],
             device_id={"seg": target}, device_id_type=MESH)
 
-    each(lambda i, peer: params_copy(2 * REACH - i, peer).start())
     for load in loads[4:]:
         load.wait()
     gates_ref[0:1, :] = fraction_ref[...]
@@ -107,7 +104,11 @@
             mig[rows, c * gates:(c + 1) * gates] = z.astype(jnp.bfloat16)
         return carry
 
-    lax.fori_loop(0, pulse_count // ROWS, migrate_rows, 0, unroll=4)
+    chunks = pulse_count // ROWS
+    lax.fori_loop(0, chunks // 2, migrate_rows, 0, unroll=4)
+    pl.semaphore_wait(barrier, jnp.minimum(me, REACH) + jnp.minimum(n - 1 - me, REACH))
+    each(lambda i, peer: params_copy(2 * REACH - i, peer).start())
+    lax.fori_loop(chunks // 2, chunks, migrate_rows, 0, unroll=4)
 
     pulse = (me * pulse_count + lax.broadcasted_iota(jnp.int32, (ROWS, pulse_count), 1)).astype(jnp.float32)
 

time: 22.3 us -> 22.9 us (1.027)
  Pallas kernels: 21.5 us -> 22 us
    pallas_call x1, Pallas kernels: 19.8 us -> 20.4 us  [shards(): pl.pallas_call(functools.partial(kernel, n), out_shape=outs, in_specs=[hb...]
where the time goes in v7:
time: 22.9 us; the launch traced here: 22.7 us
  Pallas kernels  22 us (96%)
  between operations  0.64 us (3%)
    pallas_call x1, Pallas kernels, shards(): pl.pallas_call(functools.partial(kernel, n), out_shape=outs, in_specs=[hb...  20.4 us
    pallas_call x1, Pallas kernels, shards(): pl.pallas_call(hand_over, out_shape=outs, in_specs=[hbm, hbm], out_specs=...  1.66 us

profile of v7, /device:TPU:3, one launch (start us, length us, event | category | flops | bytes accessed | tf_op | source)
XLA Modules:
  0.0 22.7 jit_solution(3802675520899757764)
XLA Ops:
  0.6 20.4 %shard_map.86 = (bf16[2,128,256]{2,1,0:T(8,128)(2,1)}, f32[128,256]{1,0:T(8,128)}) custom-call(bf16[2,256,256]{2,1,0:T(8,128)(2,1)} %pulses_hbm.1, f32[1,256]{1,0:T(1,128)} %bitcast.6, s32[1,256]{1,0:T(1,128)} %bitcast.7, s32[1,128]{1,0:T(1,128)} %bitcast.8, s32[1,128]{1,0:T(1,128)} %bitcast.9, f32[1,128]{1,0:T(1,128)} %bitcast.10, f32[1,128]{1,0:T(1,128)} %bitcast.11), custom_call_target="tpu_custom_call" | custom-call | tf_op jit(solution)/shard_map/pallas_call | solution.py:305
  21.0 1.7 %shard_map.87 = (bf16[2,128,256]{2,1,0:T(8,128)(2,1)}, f32[128,256]{1,0:T(8,128)}) custom-call(bf16[2,128,256]{2,1,0:T(8,128)(2,1)} %get-tuple-element.4.focus_in, f32[128,256]{1,0:T(8,128)} %get-tuple-element.5.look_in), custom_call_target="tpu_custom_call" | custom-call | tf_op jit(solution)/shard_map/pallas_call | solution.py:326
